TPU v7x, 128 devices: a whole 4x4x4 slice. The times are simulated.
128 devices in a mesh: dp: 8 (over x, z_hi), stream: 16 (over y, z_lo, core).
Axes of the slice: x: 4, y: 4, z: 4 (z_hi: 2, z_lo: 2; z = z_hi * 2 + z_lo), core: 2. Of those that a mesh axis runs over, the one named last changes fastest.
Arguments:
- source_embed: bfloat16 [32768, 256], P(('dp', 'stream')), may hold values from -6 to 6
- source_labels: int32 [32768], P(('dp', 'stream')), may hold values from 0 to 63
- target_embed: bfloat16 [8192, 256], P('stream'), may hold values from -6 to 6
- target_labels: int32 [8192], P('stream'), may hold values from 0 to 63
- label_table: bfloat16 [64, 64], replicated, may hold values from 0 to 2
Outputs:
- source_potential: float32 [32768], P(('dp', 'stream'))
- target_dual: float32 [8192], P('stream')
All inputs are finite; a program needn't handle non-finite values.
Results may differ from a plain program's by a relative error of at most 0.0003.
Values may be sent and summed in bfloat16 or wider, within the bound.
A program may use at most 64 MiB of HBM per device.

v0:
```python
import math

import jax
import jax.numpy as jnp
from jax import lax
from jax.sharding import PartitionSpec as P

ITERS = 3


entropic_scale = 0.02


def softmax_join(first, second):
    running_max = jnp.maximum(first[0], second[0])
    return (running_max, second[1] * jnp.exp(second[0] - running_max))


def block_terms(scores, reduce_axis):
    running_max = jnp.max(scores, axis=reduce_axis)
    exp_sum = jnp.sum(jnp.exp(scores - jnp.expand_dims(running_max, reduce_axis)), axis=reduce_axis)
    return (running_max, exp_sum)


def cross_terms(left, right):
    return lax.dot_general(
        left, right, (((1,), (1,)), ((), ())), preferred_element_type=jnp.float32
    )


def augment(embed, labels, table, transpose_table):
    width = table.shape[0]
    padded_width = (width + 127) // 128 * 128
    padded_table = jnp.pad(table, ((0, padded_width - width), (0, padded_width - width)))
    if transpose_table:
        padded_table = padded_table.T
    onehot = (labels[:, None] == jnp.arange(padded_width, dtype=jnp.int32)[None, :]).astype(
        jnp.bfloat16
    )
    label_rows = jnp.dot(onehot, padded_table, preferred_element_type=jnp.float32).astype(
        jnp.bfloat16
    )
    scale = jnp.asarray(-2.0 / embed.shape[1], jnp.bfloat16)
    left_side = jnp.concatenate([embed * scale, onehot], axis=1)
    sent_side = jnp.concatenate([embed, label_rows], axis=1)
    norms = jnp.sum(jnp.square(embed.astype(jnp.float32)), axis=1) / embed.shape[1]
    return (left_side, sent_side, norms)


def column_dual(running_max, exp_sum, log_source_weight):
    overall = lax.pmax(running_max, "dp")
    exp_sum = lax.psum(exp_sum * jnp.exp(running_max - overall), "dp")
    running_max = overall
    return -entropic_scale * (jnp.log(exp_sum) + running_max - log_source_weight)


def body(source_embed, source_labels, target_embed, target_labels, label_table):
    src_rows = source_embed.shape[0]
    tgt_rows = target_embed.shape[0]
    stream_count = lax.axis_size("stream")
    log_target_weight = math.log(tgt_rows * stream_count)
    log_source_weight = math.log(src_rows * stream_count * lax.axis_size("dp"))
    src_left, src_send, src_norm = augment(source_embed, source_labels, label_table, False)
    tgt_left, tgt_send, tgt_norm = augment(target_embed, target_labels, label_table, True)
    target_dual = jnp.zeros((tgt_rows,), jnp.float32)
    source_potential = jnp.zeros((src_rows,), jnp.float32)
    for turn in range(ITERS):
        shift_all = lax.all_gather(target_dual - tgt_norm, "stream", axis=0, tiled=True)

        def row_step(carry, piece, start, shift_all=shift_all):
            scores = (
                shift_all[None, :] - src_norm[:, None] - cross_terms(src_left, piece)
            ) / entropic_scale
            return softmax_join(carry, block_terms(scores, 1))

        row_init = (jnp.full((src_rows,), -1e30, jnp.float32), jnp.zeros((src_rows,), jnp.float32))
        running_max, exp_sum = row_step(
            row_init, lax.all_gather(tgt_send, "stream", axis=0, tiled=True), jnp.int32(0)
        )
        source_potential = -entropic_scale * (jnp.log(exp_sum) + running_max - log_target_weight)
        group_shift = lax.all_gather(source_potential - src_norm, "stream", axis=0, tiled=True)

        def column_step(carry, piece, start, group_shift=group_shift):
            scores = (
                group_shift[None, :] - tgt_norm[:, None] - cross_terms(tgt_left, piece)
            ) / entropic_scale
            return softmax_join(carry, block_terms(scores, 1))

        column_init = (
            jnp.full((tgt_rows,), -1e30, jnp.float32),
            jnp.zeros((tgt_rows,), jnp.float32),
        )
        running_max, exp_sum = column_step(
            column_init, lax.all_gather(src_send, "stream", axis=0, tiled=True), jnp.int32(0)
        )
        target_dual = column_dual(running_max, exp_sum, log_source_weight)
    return (source_potential, target_dual)


def solution(mesh):
    placed = (P(("dp", "stream"), None), P(("dp", "stream")), P("stream", None), P("stream"), P())
    return jax.shard_map(
        body,
        mesh=mesh,
        in_specs=placed,
        out_specs=(P(("dp", "stream")), P("stream")),
        check_vma=False,
    )
```

profile of v0, /device:TPU:1, one launch (start us, length us, event | category | flops | bytes accessed | tf_op | source)
XLA Modules:
  0.0 326.3 jit_solution(4753727286010131187)
XLA Ops:
  7.2 0.0 all-gather.9.cloned.1.call-start
  7.2 1.0 convolution_convert_fusion
  8.2 1.8 pad_maximum_fusion
  10.0 0.0 all-gather.9.cloned.1.call-update
  10.0 0.0 all-gather.11.cloned.1.call-start
  10.0 0.9 convolution_convert_fusion.1
  11.0 1.6 pad_maximum_fusion.1
  12.6 0.0 all-gather.11.cloned.1.call-update
  12.6 1.1 multiply_reduce_fusion
  13.7 22.0 %all-gather = f32[16,1,512]{2,1,0:T(1,128)S(1)} all-gather(f32[1,1,512]{2,1,0:T(1,128)S(1)} %bitcast.30), channel_id=1, replica_groups=mesh['dp'=8,'stream'=16] {'stream'}, dimensions={0}, use_global_device_ids=true | all-gather | bytes 34816 | tf_op jit(solution)/shard_map/all_gather | solution.py:68
  35.7 1.0 multiply_reduce_fusion.1
  36.8 0.8 fusion.16
  37.5 0.8 fusion.10
  38.4 0.9 broadcast_multiply_fusion.1
  39.3 1.0 broadcast_multiply_fusion
  40.3 16.0 %all-gather.9.cloned.1.call-done = bf16[8192,384]{1,0:T(8,128)(2,1)} async-done(((bf16[512,384]{1,0:T(8,128)(2,1)}), bf16[8192,384]{1,0:T(8,128)(2,1)}) %all-gather.9.cloned.1.call-update) | async-done | bytes 6291472 | tf_op jit(solution)/shard_map/all_gather | solution.py:78
  56.3 5.3 %fusion = (f32[256]{0:T(256)S(1)}, f32[256,8192]{1,0:T(8,128)S(1)}) fusion(f32[256]{0:T(256)S(1)} %broadcast_multiply_fusion.3, f32[8192]{0:T(1024)S(1)} %bitcast.26, bf16[8192,384]{1,0:T(8,128)(2,1)} %all-gather.9.cloned.1.call-done, bf16[256,128]{1,0:T(8,128)(2,1)S(1)} %fusion.16, bf16[256,256]{1,0:T(8,128)(2,1)S(1)} %broadcast_multiply_fusion.1), kind=kOutput, calls=%fused_computation.12 | convolution fusion | flops 1619394304 | bytes 14911488 | tf_op jit(solution)/shard_map/dot_general | solution.py:26
  61.5 3.2 copy-done
  64.8 2.3 exponential_reduce_fusion.5
  67.1 18.8 %all-gather.1 = f32[16,1,256]{2,1,0:T(1,128)S(1)} all-gather(f32[1,1,256]{2,1,0:T(1,128)S(1)} %bitcast.34), channel_id=1, replica_groups=mesh['dp'=8,'stream'=16] {'stream'}, dimensions={0}, use_global_device_ids=true | all-gather | bytes 17408 | tf_op jit(solution)/shard_map/all_gather | solution.py:81
  85.9 8.5 %all-gather.11.cloned.1.call-done = bf16[4096,384]{1,0:T(8,128)(2,1)} async-done(((bf16[256,384]{1,0:T(8,128)(2,1)}), bf16[4096,384]{1,0:T(8,128)(2,1)}) %all-gather.11.cloned.1.call-update) | async-done | bytes 3145744 | tf_op jit(solution)/shard_map/all_gather | solution.py:94
  94.4 4.4 %fusion.1 = (f32[512]{0:T(512)S(1)}, f32[512,4096]{1,0:T(8,128)S(1)}) fusion(f32[512]{0:T(512)S(1)} %get-tuple-element.5, f32[4096]{0:T(1024)S(1)} %bitcast.28, bf16[4096,384]{1,0:T(8,128)(2,1)} %all-gather.11.cloned.1.call-done, bf16[512,128]{1,0:T(8,128)(2,1)S(1)} %fusion.10, bf16[512,256]{1,0:T(8,128)(2,1)S(1)} %broadcast_multiply_fusion), kind=kOutput, calls=%fused_computation.13 | convolution fusion | flops 1619787264 | bytes 11948032 | tf_op jit(solution)/shard_map/dot_general | solution.py:26
  98.9 3.2 copy-done.1
  102.1 2.4 exponential_reduce_fusion.4
  104.5 20.4 %pmax.21 = f32[512]{0:T(512)S(1)} all-reduce(f32[512]{0:T(512)S(1)} %broadcast_maximum_fusion.2), channel_id=1, replica_groups=mesh['dp'=8,'stream'=16] {'dp'}, use_global_device_ids=true, to_apply=%region_6.7 | all-reduce | flops 512 | bytes 4096 | tf_op jit(solution)/shard_map/pmax | solution.py:51
  124.9 15.5 %psum.21 = f32[512]{0:T(512)S(1)} all-reduce(f32[512]{0:T(512)S(1)} %exponential_multiply_fusion.2), channel_id=1, replica_groups=mesh['dp'=8,'stream'=16] {'dp'}, use_global_device_ids=true, to_apply=%region_7.8 | all-reduce | flops 512 | bytes 4096 | tf_op jit(solution)/shard_map/psum | solution.py:52
  140.4 24.6 %all-gather.2 = f32[16,1,512]{2,1,0:T(1,128)S(1)} all-gather(f32[1,1,512]{2,1,0:T(1,128)S(1)} %bitcast.32), channel_id=1, replica_groups=mesh['dp'=8,'stream'=16] {'stream'}, dimensions={0}, use_global_device_ids=true | all-gather | bytes 34816 | tf_op jit(solution)/shard_map/all_gather | solution.py:68
  165.0 4.9 %fusion.2 = f32[256]{0:T(256)S(1)} fusion(f32[256,8192]{1,0:T(8,128)} %copy-done, f32[8192]{0:T(1024)S(1)} %bitcast.20, f32[256]{0:T(256)S(1)} %broadcast_multiply_fusion.3), kind=kLoop, calls=%fused_computation.14 | loop fusion | flops 8388352 | bytes 8423424 | tf_op jit(solution)/shard_map/reduce_max | solution.py:20
  169.9 4.8 %exponential_reduce_fusion.3 = f32[256]{0:T(256)S(1)} fusion(f32[256,8192]{1,0:T(8,128)} %copy-done, f32[256]{0:T(256)S(1)} %fusion.2, f32[8192]{0:T(1024)S(1)} %bitcast.21, f32[256]{0:T(256)S(1)} %broadcast_multiply_fusion.3), kind=kLoop, calls=%fused_computation.6 | loop fusion | flops 10485504 | bytes 8424448 | tf_op jit(solution)/shard_map/reduce_sum | solution.py:21
  174.7 16.9 %all-gather.3 = f32[16,1,256]{2,1,0:T(1,128)S(1)} all-gather(f32[1,1,256]{2,1,0:T(1,128)S(1)} %bitcast.35), channel_id=1, replica_groups=mesh['dp'=8,'stream'=16] {'stream'}, dimensions={0}, use_global_device_ids=true | all-gather | bytes 17408 | tf_op jit(solution)/shard_map/all_gather | solution.py:81
  191.5 0.0 slice-done
  191.5 0.0 slice-done.1
  191.5 1.2 fusion.3
  192.8 2.4 exponential_reduce_fusion.2
  195.2 18.9 %pmax.22 = f32[512]{0:T(512)S(1)} all-reduce(f32[512]{0:T(512)S(1)} %broadcast_maximum_fusion.1), channel_id=1, replica_groups=mesh['dp'=8,'stream'=16] {'dp'}, use_global_device_ids=true, to_apply=%region_12.13 | all-reduce | flops 512 | bytes 4096 | tf_op jit(solution)/shard_map/pmax | solution.py:51
  214.1 15.5 %psum.22 = f32[512]{0:T(512)S(1)} all-reduce(f32[512]{0:T(512)S(1)} %exponential_multiply_fusion.1), channel_id=1, replica_groups=mesh['dp'=8,'stream'=16] {'dp'}, use_global_device_ids=true, to_apply=%region_13.14 | all-reduce | flops 512 | bytes 4096 | tf_op jit(solution)/shard_map/psum | solution.py:52
  229.6 24.3 %all-gather.4 = f32[16,1,512]{2,1,0:T(1,128)S(1)} all-gather(f32[1,1,512]{2,1,0:T(1,128)S(1)} %bitcast.31), channel_id=1, replica_groups=mesh['dp'=8,'stream'=16] {'stream'}, dimensions={0}, use_global_device_ids=true | all-gather | bytes 34816 | tf_op jit(solution)/shard_map/all_gather | solution.py:68
  253.9 4.9 %fusion.4 = f32[256]{0:T(256)S(1)} fusion(f32[256,8192]{1,0:T(8,128)} %copy-done, f32[8192]{0:T(1024)S(1)} %bitcast.18, f32[256]{0:T(256)S(1)} %broadcast_multiply_fusion.3), kind=kLoop, calls=%fused_computation.16 | loop fusion | flops 8388352 | bytes 8423424 | tf_op jit(solution)/shard_map/reduce_max | solution.py:20
  258.8 4.8 %exponential_reduce_fusion.1 = f32[256]{0:T(256)S(1)} fusion(f32[256,8192]{1,0:T(8,128)} %copy-done, f32[256]{0:T(256)S(1)} %fusion.4, f32[8192]{0:T(1024)S(1)} %bitcast.19, f32[256]{0:T(256)S(1)} %broadcast_multiply_fusion.3), kind=kLoop, calls=%fused_computation.2 | loop fusion | flops 10485504 | bytes 8424448 | tf_op jit(solution)/shard_map/reduce_sum | solution.py:21
  263.6 0.6 fusion.33
  264.2 16.8 %all-gather.5 = f32[16,1,256]{2,1,0:T(1,128)S(1)} all-gather(f32[1,1,256]{2,1,0:T(1,128)S(1)} %bitcast.33), channel_id=1, replica_groups=mesh['dp'=8,'stream'=16] {'stream'}, dimensions={0}, use_global_device_ids=true | all-gather | bytes 17408 | tf_op jit(solution)/shard_map/all_gather | solution.py:81
  281.0 0.0 slice-done.2
  281.0 0.0 slice-done.3
  281.0 1.2 fusion.5
  282.3 2.4 exponential_reduce_fusion
  284.7 18.7 %pmax.23 = f32[512]{0:T(512)S(1)} all-reduce(f32[512]{0:T(512)S(1)} %broadcast_maximum_fusion), channel_id=1, replica_groups=mesh['dp'=8,'stream'=16] {'dp'}, use_global_device_ids=true, to_apply=%region_18.19 | all-reduce | flops 512 | bytes 4096 | tf_op jit(solution)/shard_map/pmax | solution.py:51
  303.4 15.5 %psum.23 = f32[512]{0:T(512)S(1)} all-reduce(f32[512]{0:T(512)S(1)} %exponential_multiply_fusion), channel_id=1, replica_groups=mesh['dp'=8,'stream'=16] {'dp'}, use_global_device_ids=true, to_apply=%region_19.20 | all-reduce | flops 512 | bytes 4096 | tf_op jit(solution)/shard_map/psum | solution.py:52
  318.9 0.6 add_multiply_fusion
  (20 shorter events, 0.1 us)
Async XLA Ops:
  7.2 49.1 %all-gather.9.cloned.1.call-start = ((), (), s32[]{:S(2)}) async-start(), calls=%async_computation | async-start | bytes 6684672 | tf_op jit(solution)/shard_map/all_gather | solution.py:78
  10.0 84.4 %all-gather.11.cloned.1.call-start = ((), (), s32[]{:S(2)}) async-start(), calls=%async_computation.1 | async-start | bytes 3342336 | tf_op jit(solution)/shard_map/all_gather | solution.py:94
  61.5 3.2 copy-start
  98.9 3.2 copy-start.1
  165.0 26.5 %slice-start = ((s8[8388608]{0:T(1024)(128)(4,1)}), s8[4194304]{0:T(1024)(128)(4,1)S(1)}, s32[]{:S(2)}) async-start(s8[8388608]{0:T(1024)(128)(4,1)} %bitcast.14), calls=%async_computation.2 | async-start | bytes 8388608
  169.9 21.7 %slice-start.1 = ((s8[8388608]{0:T(1024)(128)(4,1)}), s8[4194304]{0:T(1024)(128)(4,1)S(1)}, s32[]{:S(2)}) async-start(s8[8388608]{0:T(1024)(128)(4,1)} %bitcast.14), calls=%async_computation.3 | async-start | bytes 8388608
  253.9 27.1 %slice-start.2 = ((s8[8388608]{0:T(1024)(128)(4,1)}), s8[4194304]{0:T(1024)(128)(4,1)S(1)}, s32[]{:S(2)}) async-start(s8[8388608]{0:T(1024)(128)(4,1)} %bitcast.16), calls=%async_computation.4 | async-start | bytes 8388608
  258.8 22.2 %slice-start.3 = ((s8[8388608]{0:T(1024)(128)(4,1)}), s8[4194304]{0:T(1024)(128)(4,1)S(1)}, s32[]{:S(2)}) async-start(s8[8388608]{0:T(1024)(128)(4,1)} %bitcast.16), calls=%async_computation.5 | async-start | bytes 8388608
Sparse Core Ops, SparseCore 0:
  10.1 46.1 all-gather.8
  58.0 36.4 all-gather.10
where the time goes:
time: 333 us; the launch traced here: 326 us
  blocking collectives  228 us (68%)
  other arithmetic  41.6 us (12%)
  waiting for transfers between devices  24.5 us (7%)
  between operations  14.2 us (4%)
  matrix products  11.7 us (4%)
  local copies, waits for them, and re-layouts  6.44 us (2%)
    all_gather x3, blocking collectives, body(): lax.all_gather(target_dual - tgt_norm, 'stream', axis=0, tiled=True)  70.9 us
    pmax x3, blocking collectives, column_dual(): overall = lax.pmax(running_max, 'dp')  58 us
    all_gather x3, blocking collectives, body(): lax.all_gather(source_potential - src_norm, 'stream', axis=0, tiled=True)  52.5 us
    psum x3, blocking collectives, column_dual(): exp_sum = lax.psum(exp_sum * jnp.exp(running_max - overall), 'dp')  46.4 us
    reduce_sum x6, other arithmetic, block_terms(): jnp.sum(jnp.exp(scores - jnp.expand_dims(running_max, reduce_axis)), axis...  19.1 us
    all_gather x1, waiting for transfers between devices, body(): lax.all_gather(tgt_send, 'stream', axis=0, tiled=True)  16 us
    reduce_max x4, other arithmetic, block_terms(): running_max = jnp.max(scores, axis=reduce_axis)  12.2 us
    dot_general x2, matrix products, cross_terms(): lax.dot_general(left, right, (((1,), (1,)), ((), ())), preferred_element_...  9.72 us
  transfers between devices with their start and end apart: 2, of which 2 were waited for; matrix products, arithmetic and copies ran while one was open for 5% of the time, Pallas kernels for 0%

commit v1 on v0

v1 whole, which is shorter than its diff:
```python
import functools
import math

import jax
import jax.numpy as jnp
from jax import lax
from jax.experimental import pallas as pl
from jax.experimental.pallas import tpu as pltpu
from jax.sharding import PartitionSpec as P

MESH = pl.DeviceIdType.MESH
SCALE = 0.02
LOG2E = 1.0 / math.log(2.0)
COST_TO_BITS = LOG2E / SCALE

SRC = 256
TGT = 512
EMB = 256
LABELS = 64
AUX = 16
CHUNKS = 8
QUARTERS = 4
ROWS = QUARTERS * 256
COLS = CHUNKS * SRC
LANES = 128
TILES = COLS // LANES
NT = (((1,), (1,)), ((), ()))


def place():
    dp, stream = lax.axis_index("dp"), lax.axis_index("stream")
    return dp // 2, stream // 4, (dp % 2) * 2 + (stream // 2) % 2, stream % 2


def device(x, y, z, core):
    x, y, z, core = x % 4, y % 4, z % 4, core % 2
    return (x * 2 + z // 2, y * 4 + (z % 2) * 2 + core)


def split3(value):
    high = value.astype(jnp.bfloat16).astype(jnp.float32)
    rest = value - high
    middle = rest.astype(jnp.bfloat16).astype(jnp.float32)
    return high, middle, rest - middle


def aux_rows(embed, labels):
    wide = embed.astype(jnp.float32)
    square = wide * wide
    high = square.astype(jnp.bfloat16)
    low = (square - high.astype(jnp.float32)).astype(jnp.bfloat16)
    ones = jnp.ones((AUX, EMB), jnp.bfloat16)
    norm = lax.dot_general(ones, high, NT, preferred_element_type=jnp.float32)
    norm += lax.dot_general(ones, low, NT, preferred_element_type=jnp.float32)
    first, second, third = split3(norm * (-128.0 / EMB))
    row = lax.broadcasted_iota(jnp.int32, (AUX, SRC), 0)
    marks = jnp.broadcast_to(labels.astype(jnp.float32), (AUX, SRC))
    out = jnp.where(row == 0, marks, 0.0)
    out = jnp.where(row == 1, first, out)
    out = jnp.where(row == 2, second, out)
    out = jnp.where(row == 3, third, out)
    return out.astype(jnp.bfloat16)


def kernel(
    src_ref, src_labels, tgt_ref, tgt_labels, table, f_out, g_out,
    src, tgt, src_side, tgt_side, block, peak, col_max, weight, weight_now, partial,
    spread, s_msg, t_msg, f_first, g_first,
    in_sem, gather_send, gather_recv, s_send, s_recv, t_send, t_recv,
):
    x, y, z, core = place()
    z_lo = z % 2
    mine = y * 2 + core
    s_peers = [(dy, dc) for dy in range(4) for dc in range(2) if (dy, dc) != (0, 0)]
    t_peers = [(dx, dz) for dx in range(4) for dz in range(4) if (dx, dz) != (0, 0)]
    f32 = jnp.float32

    barrier = pltpu.get_barrier_semaphore()
    for dy, dc in s_peers:
        pl.semaphore_signal(barrier, inc=1, device_id=device(x, y + dy, z, core + dc), device_id_type=MESH)
    for dx, dz in t_peers:
        pl.semaphore_signal(barrier, inc=1, device_id=device(x + dx, y, z + dz, core), device_id_type=MESH)

    loads = [
        pltpu.make_async_copy(src_ref, src.at[mine, pl.ds(0, SRC)], in_sem.at[0]),
        pltpu.make_async_copy(tgt_ref.at[pl.ds(0, 256)], tgt.at[2 * z_lo, pl.ds(0, 256)], in_sem.at[1]),
        pltpu.make_async_copy(tgt_ref.at[pl.ds(256, 256)], tgt.at[2 * z_lo + 1, pl.ds(0, 256)], in_sem.at[2]),
    ]
    for load in loads:
        load.start()
    for load in loads:
        load.wait()
    src[mine, pl.ds(SRC, AUX)] = aux_rows(src[mine, pl.ds(0, SRC)], src_labels[...])
    for half in range(2):
        tgt[2 * z_lo + half, pl.ds(256, AUX)] = aux_rows(
            tgt[2 * z_lo + half, pl.ds(0, 256)], tgt_labels[:, half * 256 : half * 256 + 256]
        )

    pl.semaphore_wait(barrier, len(s_peers) + len(t_peers))

    def send(ref_from, ref_to, k, target):
        copy = pltpu.make_async_remote_copy(
            src_ref=ref_from, dst_ref=ref_to, send_sem=gather_send.at[k], recv_sem=gather_recv.at[k],
            device_id=target, device_id_type=MESH,
        )
        copy.start()
        return copy

    started = [send(src.at[mine], src.at[mine], 0, device(x, y, z, core + 1))]
    started += [send(tgt.at[2 * z_lo + h], tgt.at[2 * z_lo + h], 7 + h, device(x, y, z + 1 - 2 * h, core)) for h in range(2)]
    started += [send(src.at[mine], src.at[mine], k, device(x, y + k, z, core)) for k in (1, 3, 2)]

    def arrived(ref, k):
        pltpu.make_async_copy(ref, ref, gather_recv.at[k]).wait()

    def prepare_source(chunk):
        aux = src[chunk, pl.ds(SRC, AUX)].astype(f32)
        row = lax.broadcasted_iota(jnp.int32, (LANES, SRC), 0)
        side = jnp.where(row.astype(f32) == aux[0:1], 1.0, 0.0)
        side = jnp.where((row >= 67) & (row < 70), 1.0, side)
        for k in range(3):
            side = jnp.where(row == LABELS + k, aux[1 + k : 2 + k], side)
        src_side[chunk] = side.astype(jnp.bfloat16)

    def prepare_target(quarter):
        aux = tgt[quarter, pl.ds(256, AUX)].astype(f32)
        row = lax.broadcasted_iota(jnp.int32, (LABELS, 256), 0)
        onehot = jnp.where(row.astype(f32) == aux[0:1], 1.0, 0.0).astype(jnp.bfloat16)
        costs = jnp.dot(table[...], onehot, preferred_element_type=f32) * -128.0
        rest = jnp.where(row < 3, 1.0, 0.0)
        for k in range(3):
            rest = jnp.where(row == 3 + k, aux[1 + k : 2 + k], rest)
        tgt_side[quarter] = jnp.concatenate([costs, rest], axis=0).T.astype(jnp.bfloat16)

    def cols_of(chunk):
        return pl.ds(pl.multiple_of(chunk * SRC, SRC), SRC)

    def costs(quarter, chunk):
        dot = lax.dot_general(tgt[quarter, pl.ds(0, 256)], src[chunk, pl.ds(0, SRC)], NT, preferred_element_type=f32)
        dot += jnp.dot(tgt_side[quarter], src_side[chunk], preferred_element_type=f32)
        dot = dot * (COST_TO_BITS / 128.0)
        block[pl.ds(pl.multiple_of(quarter * 256, 256), 256), cols_of(chunk)] = dot
        peak[quarter, :, cols_of(chunk)] = jnp.max(dot.reshape(32, 8, SRC), axis=0)

    def first_rows(chunk):
        top = jnp.max(jnp.max(peak[:, :, cols_of(chunk)], axis=0), axis=0, keepdims=True)

        def add(step, total):
            rows = pl.ds(pl.multiple_of(step * 32, 32), 32)
            return total + jnp.exp2(block[rows, cols_of(chunk)] - top)

        total = lax.fori_loop(0, ROWS // 32, add, jnp.zeros((32, SRC), f32), unroll=4)
        s_msg[0, 0, pl.ds(chunk, 1)] = top + jnp.log2(jnp.sum(total, axis=0, keepdims=True))

    own, other = mine, y * 2 + (1 - core)
    prepare_source(own)
    for half in range(2):
        prepare_target(2 * z_lo + half)
        costs(2 * z_lo + half, own)
    arrived(src.at[other], 0)
    prepare_source(other)
    for half in range(2):
        costs(2 * z_lo + half, other)
    away = 2 * (1 - z_lo)
    for half in range(2):
        arrived(tgt.at[away + half], 7 + half)
        prepare_target(away + half)
        costs(away + half, own)
        costs(away + half, other)
    first_rows(own)
    first_rows(other)

    def whole_chunk(chunk):
        prepare_source(chunk)
        for quarter in range(QUARTERS):
            costs(quarter, chunk)
        first_rows(chunk)

    def chunk_at(k, c):
        return ((y - k) % 4) * 2 + c

    def take(k):
        chunk = chunk_at(k, core)
        arrived(src.at[chunk], k)
        started.append(send(src.at[chunk], src.at[chunk], 3 + k, device(x, y, z, core + 1)))

    take(1)
    take(3)
    whole_chunk(chunk_at(1, core))
    whole_chunk(chunk_at(3, core))
    for k in (1, 3):
        arrived(src.at[chunk_at(k, 1 - core)], 3 + k)
        whole_chunk(chunk_at(k, 1 - core))
    take(2)
    whole_chunk(chunk_at(2, core))
    arrived(src.at[chunk_at(2, 1 - core)], 5)
    whole_chunk(chunk_at(2, 1 - core))

    def exchange_s(turn):
        for dy, dc in s_peers:
            pltpu.make_async_remote_copy(
                src_ref=s_msg.at[turn, 0], dst_ref=s_msg.at[turn, dy * 2 + dc],
                send_sem=s_send.at[turn], recv_sem=s_recv.at[turn],
                device_id=device(x, y + dy, z, core + dc), device_id_type=MESH,
            ).start()
        others = s_msg.at[turn, pl.ds(1, 7)]
        pltpu.make_async_copy(others, others, s_recv.at[turn]).wait()

    def exchange_t(turn):
        for dx, dz in t_peers:
            pltpu.make_async_remote_copy(
                src_ref=t_msg.at[turn, 0], dst_ref=t_msg.at[turn, dx * 4 + dz],
                send_sem=t_send.at[turn], recv_sem=t_recv.at[turn],
                device_id=device(x + dx, y, z + dz, core), device_id_type=MESH,
            ).start()
        others = t_msg.at[turn, pl.ds(1, 15)]
        pltpu.make_async_copy(others, others, t_recv.at[turn]).wait()

    def joined(parts):
        top = jnp.max(parts, axis=0)
        return top + jnp.log2(jnp.sum(jnp.exp2(parts - top), axis=0))

    def spread_rows(values):
        for chunk in range(CHUNKS):
            spread[:, chunk * SRC : (chunk + 1) * SRC] = jnp.broadcast_to(values[chunk : chunk + 1], (8, SRC))

    def tile(l):
        return slice(l * LANES, (l + 1) * LANES)

    def as_columns(values, b):
        return jnp.broadcast_to(values[b : b + 1], (LANES, LANES)).T

    exchange_s(0)
    source_count = COLS * 16.0
    target_count = ROWS * 8.0
    f_now = math.log2(target_count) - joined(s_msg[0])
    f_first[...] = f_now
    spread_rows(f_now)

    def first_columns(step, _):
        tops = []
        for s in range(4):
            rows = pl.ds(pl.multiple_of(step * 32 + s * 8, 8), 8)
            top = block[rows, tile(0)] + spread[:, tile(0)]
            for l in range(1, TILES):
                top = jnp.maximum(top, block[rows, tile(l)] + spread[:, tile(l)])
            tops.append(jnp.max(top, axis=1, keepdims=True))
        for s in range(4):
            rows = pl.ds(pl.multiple_of(step * 32 + s * 8, 8), 8)
            top = jnp.broadcast_to(tops[s], (8, LANES))
            total = jnp.zeros((8, LANES), f32)
            for l in range(TILES):
                value = jnp.exp2(block[rows, tile(l)] + (spread[:, tile(l)] - top))
                block[rows, tile(l)] = value
                total = total + value
            col_max[rows, :] = top
            partial[rows, :] = top + jnp.log2(jnp.sum(total, axis=1, keepdims=True))
        return 0

    lax.fori_loop(0, ROWS // 32, first_columns, 0)
    for b in range(8):
        t_msg[0, 0, b : b + 1] = partial[b * LANES : (b + 1) * LANES, :].T[0:1]
    exchange_t(0)
    g_now = math.log2(source_count) - joined(t_msg[0])
    g_first[...] = g_now
    for b in range(8):
        rows = slice(b * LANES, (b + 1) * LANES)
        weight[rows, :] = jnp.exp2(col_max[rows, :] + as_columns(g_now, b))

    def row_sums(weights, turn):
        def add(step, totals):
            for s in range(4):
                rows = pl.ds(pl.multiple_of(step * 32 + s * 8, 8), 8)
                w = weights[rows, :]
                totals = tuple(totals[l] + block[rows, tile(l)] * w for l in range(TILES))
            return totals

        totals = lax.fori_loop(0, ROWS // 32, add, tuple(jnp.zeros((8, LANES), f32) for _ in range(TILES)))
        for l in range(TILES):
            s_msg[turn, 0, l // 2 : l // 2 + 1, tile(l % 2)] = jnp.sum(totals[l], axis=0, keepdims=True)

    def column_sums(turn):
        def add(step, _):
            for s in range(4):
                rows = pl.ds(pl.multiple_of(step * 32 + s * 8, 8), 8)
                total = block[rows, tile(0)] * spread[:, tile(0)]
                for l in range(1, TILES):
                    total = total + block[rows, tile(l)] * spread[:, tile(l)]
                partial[rows, :] = total * weight[rows, :]
            return 0

        lax.fori_loop(0, ROWS // 32, add, 0)
        for b in range(8):
            t_msg[turn, 0, b : b + 1] = jnp.sum(partial[b * LANES : (b + 1) * LANES, :].T, axis=0, keepdims=True)

    for turn in (1, 2):
        row_sums(weight if turn == 1 else weight_now, turn)
        exchange_s(turn)
        u_now = target_count / jnp.sum(s_msg[turn], axis=0)
        spread_rows(u_now)
        column_sums(turn)
        exchange_t(turn)
        v_now = source_count / jnp.sum(t_msg[turn], axis=0)
        if turn == 1:
            for b in range(8):
                rows = slice(b * LANES, (b + 1) * LANES)
                weight_now[rows, :] = weight[rows, :] * as_columns(v_now, b)

    f_first[...] = (f_first[...] + jnp.log2(u_now)) * (1.0 / COST_TO_BITS)
    f_out[...] = f_first[pl.ds(mine, 1)]
    g_first[...] = (g_first[...] + jnp.log2(v_now)) * (1.0 / COST_TO_BITS)
    g_out[...] = g_first[pl.ds(z_lo * 4, 4)]

    for copy in started:
        copy.wait_send()
    for turn in range(3):
        others = s_msg.at[turn, pl.ds(1, 7)]
        pltpu.make_async_copy(others, others, s_send.at[turn]).wait()
        others = t_msg.at[turn, pl.ds(1, 15)]
        pltpu.make_async_copy(others, others, t_send.at[turn]).wait()


def body(source_embed, source_labels, target_embed, target_labels, label_table):
    vmem, hbm = pl.BlockSpec(memory_space=pltpu.VMEM), pl.BlockSpec(memory_space=pl.ANY)
    f32, bf16, dma = jnp.float32, jnp.bfloat16, pltpu.SemaphoreType.DMA
    f, g = pl.pallas_call(
        kernel,
        out_shape=(jax.ShapeDtypeStruct((1, SRC), f32), jax.ShapeDtypeStruct((4, LANES), f32)),
        in_specs=[hbm, vmem, hbm, vmem, vmem],
        out_specs=(vmem, vmem),
        scratch_shapes=[
            pltpu.VMEM((CHUNKS, SRC + AUX, EMB), bf16),
            pltpu.VMEM((QUARTERS, 256 + AUX, EMB), bf16),
            pltpu.VMEM((CHUNKS, LANES, SRC), bf16),
            pltpu.VMEM((QUARTERS, 256, LANES), bf16),
            pltpu.VMEM((ROWS, COLS), f32),
            pltpu.VMEM((QUARTERS, 8, COLS), f32),
            pltpu.VMEM((ROWS, LANES), f32),
            pltpu.VMEM((ROWS, LANES), f32),
            pltpu.VMEM((ROWS, LANES), f32),
            pltpu.VMEM((ROWS, LANES), f32),
            pltpu.VMEM((8, COLS), f32),
            pltpu.VMEM((3, 8, CHUNKS, SRC), f32),
            pltpu.VMEM((3, 16, 8, LANES), f32),
            pltpu.VMEM((CHUNKS, SRC), f32),
            pltpu.VMEM((8, LANES), f32),
            dma((3,)),
            dma((9,)),
            dma((9,)),
            dma((3,)),
            dma((3,)),
            dma((3,)),
            dma((3,)),
        ],
        compiler_params=pltpu.CompilerParams(collective_id=0, has_side_effects=True, vmem_limit_bytes=40 << 20),
    )(
        source_embed,
        source_labels.reshape(1, SRC),
        target_embed,
        target_labels.reshape(1, TGT),
        label_table,
    )
    return f.reshape(SRC), g.reshape(TGT)


def solution(mesh):
    placed = (P(("dp", "stream"), None), P(("dp", "stream")), P("stream", None), P("stream"), P())
    return jax.shard_map(
        body,
        mesh=mesh,
        in_specs=placed,
        out_specs=(P(("dp", "stream")), P("stream")),
        check_vma=False,
    )
```

time: 333 us -> 62.2 us (0.19); the launches traced: 326 us -> 61.9 us
  blocking collectives: 228 us -> 0 us
  Pallas kernels: 0 us -> 56.9 us
  other arithmetic: 41.6 us -> 0 us
  waiting for transfers between devices: 24.5 us -> 0 us
  between operations: 14.2 us -> 0.66 us
  matrix products: 11.7 us -> 0 us
    all_gather x6 -> x0, blocking collectives: 123 us -> none  [the longest x3 70.9 us: body(): lax.all_gather(target_dual - tgt_norm, 'stream', axis=0, tiled=True)]
    pmax x3 -> x0, blocking collectives: 58 us -> none  [column_dual(): overall = lax.pmax(running_max, 'dp')]
    pallas_call x0 -> x1, Pallas kernels: none -> 56.9 us  [body(): pl.pallas_call(kernel, out_shape=(jax.ShapeDtypeStruct((1, SRC), f32), ja...]
    psum x3 -> x0, blocking collectives: 46.4 us -> none  [column_dual(): exp_sum = lax.psum(exp_sum * jnp.exp(running_max - overall), 'dp')]
    all_gather x2 -> x0, waiting for transfers between devices: 24.5 us -> none  [the longest x1 16 us: body(): lax.all_gather(tgt_send, 'stream', axis=0, tiled=True)]
    reduce_sum x8 -> x0, other arithmetic: 21.2 us -> none  [the longest x6 19.1 us: block_terms(): jnp.sum(jnp.exp(scores - jnp.expand_dims(running_max, reduce_axis)), axis...]
    reduce_max x4 -> x0, other arithmetic: 12.2 us -> none  [block_terms(): running_max = jnp.max(scores, axis=reduce_axis)]
    dot_general x4 -> x0, matrix products: 11.7 us -> none  [the longest x2 9.72 us: cross_terms(): lax.dot_general(left, right, (((1,), (1,)), ((), ())), preferred_element_...]
  transfers between devices with their start and end apart: 2 -> 0, of which waited for: 2 -> 0; matrix products, arithmetic and copies ran while one was open for 5% -> 0% of each run, Pallas kernels for 0% -> 0%
where the time goes in v1:
time: 62.2 us; the launch traced here: 61.9 us
  Pallas kernels  56.9 us (91%)
  local copies, waits for them, and re-layouts  4.39 us (7%)
  between operations  0.66 us (1%)
    pallas_call x1, Pallas kernels, body(): pl.pallas_call(kernel, out_shape=(jax.ShapeDtypeStruct((1, SRC), f32), ja...  56.9 us
    unnamed x12, local copies, waits for them, and re-layouts  4.39 us

profile of v1, /device:TPU:1, one launch (start us, length us, event | category | flops | bytes accessed | tf_op | source)
XLA Modules:
  0.0 61.9 jit_solution(1535049575132711634)
XLA Ops:
  0.6 0.0 copy-start.3
  0.6 0.0 copy-start.4
  0.7 0.7 %copy-done.3 = s32[512]{0:T(512)S(1)} copy-done((s32[512]{0:T(512)S(1)}, s32[512]{0:T(512)}, u32[]{:S(2)}) %copy-start.3) | copy-done | bytes 2072
  1.3 0.0 copy-done.4
  1.3 0.0 copy-start
  1.3 0.9 %copy-done = bf16[512,256]{1,0:T(8,128)(2,1)S(1)} copy-done((bf16[512,256]{1,0:T(8,128)(2,1)S(1)}, bf16[512,256]{1,0:T(8,128)(2,1)}, u32[]{:S(2)}) %copy-start) | copy-done | bytes 262168
  2.3 0.0 copy-start.1
  2.3 0.9 %copy-done.1 = bf16[256,256]{1,0:T(8,128)(2,1)S(1)} copy-done((bf16[256,256]{1,0:T(8,128)(2,1)S(1)}, bf16[256,256]{1,0:T(8,128)(2,1)}, u32[]{:S(2)}) %copy-start.1) | copy-done | bytes 131096
  3.2 0.0 copy-start.2
  3.2 0.7 %copy-done.2 = bf16[64,64]{1,0:T(8,128)(2,1)S(1)} copy-done((bf16[64,64]{1,0:T(8,128)(2,1)S(1)}, bf16[64,64]{1,0:T(8,128)(2,1)}, u32[]{:S(2)}) %copy-start.2) | copy-done | bytes 8216
  3.9 56.9 %shard_map.68 = (f32[1,256]{1,0:T(1,128)S(1)}, f32[4,128]{1,0:T(4,128)S(1)}) custom-call(bf16[256,256]{1,0:T(8,128)(2,1)S(1)} %copy-done.1, s32[1,256]{1,0:T(1,128)S(1)} %bitcast.6, bf16[512,256]{1,0:T(8,128)(2,1)S(1)} %copy-done, s32[1,512]{1,0:T(1,128)S(1)} %bitcast.4, bf16[64,64]{1,0:T(8,128)(2,1)S(1)} %copy-done.2), custom_call_target="tpu_custom_call" | custom-call | tf_op jit(solution)/shard_map/pallas_call | solution.py:326
  60.8 0.6 copy.9
  61.4 0.6 copy.10
Async XLA Ops:
  0.6 0.7 %copy-start.3 = (s32[512]{0:T(512)S(1)}, s32[512]{0:T(512)}, u32[]{:S(2)}) copy-start(s32[512]{0:T(512)} %param.8) | copy-start | bytes 6148
  0.6 0.7 %copy-start.4 = (s32[256]{0:T(256)S(1)}, s32[256]{0:T(256)}, u32[]{:S(2)}) copy-start(s32[256]{0:T(256)} %param.6) | copy-start | bytes 3076
  1.3 0.9 %copy-start = (bf16[512,256]{1,0:T(8,128)(2,1)S(1)}, bf16[512,256]{1,0:T(8,128)(2,1)}, u32[]{:S(2)}) copy-start(bf16[512,256]{1,0:T(8,128)(2,1)} %tgt_ref.1) | copy-start | bytes 786436
  2.3 0.9 %copy-start.1 = (bf16[256,256]{1,0:T(8,128)(2,1)S(1)}, bf16[256,256]{1,0:T(8,128)(2,1)}, u32[]{:S(2)}) copy-start(bf16[256,256]{1,0:T(8,128)(2,1)} %src_ref.1) | copy-start | bytes 393220
  3.2 0.7 %copy-start.2 = (bf16[64,64]{1,0:T(8,128)(2,1)S(1)}, bf16[64,64]{1,0:T(8,128)(2,1)}, u32[]{:S(2)}) copy-start(bf16[64,64]{1,0:T(8,128)(2,1)} %table.1) | copy-start | bytes 24580
